TPU v7x, 128 devices: a whole 4x4x4 slice. The times are simulated.
128 devices in a mesh: mode: 8 (over y, x_hi), col: 16 (over x_lo, z, core).
Axes of the slice: x: 4 (x_hi: 2, x_lo: 2; x = x_hi * 2 + x_lo), y: 4, z: 4, core: 2. Of those that a mesh axis runs over, the one named last changes fastest.
Arguments:
- fields: float32 [2, 288, 64, 4096], P(None, 'mode', None, 'col'), may hold values from -6 to 6
- evaluate: bfloat16 [1584, 288], replicated, may hold values from -0.375 to 0.375
- project: bfloat16 [288, 1584], replicated, may hold values from -0.15625 to 0.15625
- feed: float32 [1584], replicated, may hold values from 0.02 to 0.2
- kill: float32 [1584], replicated, may hold values from 0.04 to 0.4
Outputs:
- stepped: float32 [2, 288, 64, 4096], P(None, 'mode', None, 'col')
All inputs are finite; a program needn't handle non-finite values.
Results may differ from a plain program's by a relative error of at most 0.0039.
Values may be sent and summed in bfloat16 or wider, within the bound.
A program may use at most 384 MiB of HBM per device.

v0:
```python
import math

import jax
import jax.numpy as jnp
from jax import lax
from jax.sharding import PartitionSpec as P

SWEEPS = 4


TIME_STEP = 0.5
DIFFUSION = (1.0, 0.5)


def padded_2(cells, sides, width):
    for axis, dim in sides:
        count = lax.axis_size(axis)
        head = lax.slice_in_dim(cells, 0, width, axis=dim)
        tail = lax.slice_in_dim(cells, cells.shape[dim] - width, cells.shape[dim], axis=dim)
        cells = jnp.concatenate(
            [
                lax.ppermute(tail, axis, [(i, (i + 1) % count) for i in range(count)]),
                cells,
                lax.ppermute(head, axis, [((i + 1) % count, i) for i in range(count)]),
            ],
            axis=dim,
        )
    return cells


def react_sources(block, eval_parts, proj_parts, feed, kill):
    groups = block.shape[1]
    at_points = jnp.einsum(
        "qi,fsin->fsqn", eval_parts[0], block[:, 0], preferred_element_type=jnp.float32
    )
    for group_index in range(1, groups):
        at_points = at_points + jnp.einsum(
            "qi,fsin->fsqn",
            eval_parts[group_index],
            block[:, group_index],
            preferred_element_type=jnp.float32,
        )
    u_val = at_points[0]
    v_val = at_points[1]
    feed_col = feed[None, :, None]
    kill_col = kill[None, :, None]
    squared = u_val * v_val * v_val
    reacted = jnp.stack(
        [-squared + feed_col * (1.0 - u_val), squared - (feed_col + kill_col) * v_val]
    ).astype(jnp.bfloat16)
    outputs = [
        jnp.einsum(
            "iq,fsqn->fsin", proj_parts[group_index], reacted, preferred_element_type=jnp.float32
        )
        for group_index in range(groups)
    ]
    return jnp.stack(outputs, axis=1)


def react_all(received, evaluate, project, feed, kill):
    field_count, groups, sources, local_modes, piece_len = received.shape
    eval_parts = [evaluate[:, g * local_modes : (g + 1) * local_modes] for g in range(groups)]
    proj_parts = [project[g * local_modes : (g + 1) * local_modes, :] for g in range(groups)]
    block_count = math.gcd(4, sources)
    block_len = sources // block_count
    results = []
    for block_index in range(block_count):
        block = received[:, :, block_index * block_len : (block_index + 1) * block_len]
        results.append(react_sources(block, eval_parts, proj_parts, feed, kill))
    return jnp.concatenate(results, axis=2)


def body(fields, evaluate, project, feed, kill):
    field_count, local_modes, row_count, col_count = fields.shape
    cell_count = row_count * col_count
    groups = lax.axis_size("mode")
    rounded = fields.astype(jnp.bfloat16).reshape(field_count, 1, local_modes, cell_count)
    sources = lax.axis_size("col")
    received = lax.all_to_all(rounded, ("mode", "col"), split_axis=3, concat_axis=1, tiled=True)
    piece_len = received.shape[3]
    received = received.reshape(field_count, groups, sources, local_modes, piece_len)
    projected = react_all(received, evaluate, project, feed, kill)
    projected = projected.reshape(field_count, groups * sources, local_modes, piece_len)
    projected = lax.all_to_all(projected, ("mode", "col"), split_axis=1, concat_axis=3, tiled=True)
    projected = projected.reshape(field_count, local_modes, row_count, col_count)
    right_side = fields + TIME_STEP * projected
    weights = jnp.array(DIFFUSION, jnp.float32).reshape(2, 1, 1, 1)
    iterate = right_side
    for sweep_index in range(SWEEPS):
        extended = padded_2(iterate, (("col", 3),), 1)
        padded = jnp.pad(iterate, ((0, 0), (0, 0), (1, 1), (0, 0)))
        neighbours = (
            extended[:, :, :, 2:]
            + extended[:, :, :, :-2]
            + padded[:, :, 2:, :]
            + padded[:, :, :-2, :]
        )
        iterate = (right_side + weights * neighbours) / (1.0 + 4.0 * weights)
    return iterate


def solution(mesh):
    in_specs = (P(None, "mode", None, "col"), P(), P(), P(), P())
    out_specs = P(None, "mode", None, "col")
    return jax.shard_map(body, mesh=mesh, in_specs=in_specs, out_specs=out_specs, check_vma=False)
```

profile of v0, /device:TPU:0, one launch (start us, length us, event | category | flops | bytes accessed | tf_op | source)
XLA Modules:
  0.0 534.2 jit_solution(12619691793295813233)
XLA Ops:
  2.7 9.8 %copy.243 = bf16[2,36,64,256]{1,0,3,2:T(2,128)(2,1)} copy(bf16[2,36,64,256]{3,2,1,0:T(8,128)(2,1)S(1)} %convert_element_type.12) | data formatting | bytes 4718592 | tf_op jit(solution)/shard_map/reshape | solution.py:77
  12.5 28.2 %reshape.44 = bf16[128,2,4608]{2,1,0:T(2,128)(2,1)} reshape(bf16[16384,1,2,36]{3,2,1,0:T(2,128)(2,1)} %bitcast.520) | data formatting | bytes 4718592
  40.7 11.1 %all-to-all-start = ((bf16[128,2,4608]{2,1,0:T(2,128)(2,1)}), bf16[128,2,4608]{2,1,0:T(2,128)(2,1)S(1)}, u32[]{:S(2)}, u32[]{:S(2)}) async-start(bf16[128,2,4608]{2,1,0:T(2,128)(2,1)} %reshape.44), calls=%async_computation | async-start | bytes 4718592 | tf_op jit(solution)/shard_map/all_to_all | solution.py:79
  51.9 33.2 %all-to-all-done = bf16[128,2,4608]{2,1,0:T(2,128)(2,1)S(1)} async-done(((bf16[128,2,4608]{2,1,0:T(2,128)(2,1)}), bf16[128,2,4608]{2,1,0:T(2,128)(2,1)S(1)}, u32[]{:S(2)}, u32[]{:S(2)}) %all-to-all-start) | async-done | bytes 2359328 | tf_op jit(solution)/shard_map/all_to_all | solution.py:79
  85.1 24.9 %reshape.45 = bf16[16384,1,2,36]{3,2,1,0:T(2,128)(2,1)} reshape(bf16[128,2,4608]{2,1,0:T(2,128)(2,1)S(1)} %all-to-all-done) | data formatting | bytes 4718592
  110.0 12.5 %copy.210 = bf16[2,1,36,128,128]{4,3,0,2,1:T(8,128)(2,1)S(1)} copy(bf16[2,1,36,128,128]{2,0,4,3,1:T(2,128)(2,1)} %bitcast.521) | data formatting | bytes 4718592 | tf_op jit(solution)/shard_map/all_to_all | solution.py:79
  142.6 3.8 fusion.142
  146.4 3.8 fusion.94
  157.6 3.8 fusion.116
  165.2 3.8 fusion.132
  172.8 16.5 %fusion.92 = f32[2,4,128,1584]{2,3,1,0:T(8,128)} fusion(bf16[1584,288]{0,1:T(8,128)(2,1)S(1)} %copy-done.4, bf16[2,1,4,36,128]{4,2,1,0,3:T(4,128)(2,1)S(1)} %get-tuple-element.22), kind=kOutput, calls=%fused_computation.162 | convolution fusion | flops 116785152 | bytes 6694912 | tf_op jit(solution)/shard_map/qi,fsin->fsqn/dot_general | solution.py:37
  193.0 3.8 fusion.96
  200.6 3.9 fusion.120
  211.9 3.8 fusion.144
  219.5 3.8 fusion.114
  227.0 3.8 fusion.130
  242.1 18.2 %add_bitcast_fusion.1 = f32[2,4,1584,128]{3,2,1,0:T(8,128)} fusion(f32[2,4,128,1584]{2,3,1,0:T(8,128)} %fusion.94, f32[2,4,128,1584]{2,3,1,0:T(8,128)} %fusion.102, f32[2,4,128,1584]{2,3,1,0:T(8,128)} %fusion.110, f32[2,4,128,1584]{2,3,1,0:T(8,128)} %fusion.118, f32[2,4,128,1584]{2,3,1,0:T(8,128)} %fusion.126, f32[2,4,128,1584]{2,3,1,0:T(8,128)} %fusion.142, ...), kind=kOutput, calls=%fused_computation.1 | convolution fusion | flops 128139264 | bytes 52111360 | tf_op jit(solution)/shard_map/qi,fsin->fsqn/dot_general | solution.py:37
  260.3 18.0 %add_bitcast_fusion = f32[2,4,1584,128]{3,2,1,0:T(8,128)} fusion(f32[2,4,128,1584]{2,3,1,0:T(8,128)} %fusion.92, f32[2,4,128,1584]{2,3,1,0:T(8,128)} %fusion.100, f32[2,4,128,1584]{2,3,1,0:T(8,128)} %fusion.108, f32[2,4,128,1584]{2,3,1,0:T(8,128)} %fusion.116, f32[2,4,128,1584]{2,3,1,0:T(8,128)} %fusion.124, f32[2,4,128,1584]{2,3,1,0:T(8,128)} %fusion.140, ...), kind=kOutput, calls=%fused_computation | convolution fusion | flops 128139264 | bytes 52111360 | tf_op jit(solution)/shard_map/qi,fsin->fsqn/dot_general | solution.py:37
  278.3 18.2 %add_bitcast_fusion.2 = f32[2,4,1584,128]{3,2,1,0:T(8,128)} fusion(f32[2,4,128,1584]{2,3,1,0:T(8,128)} %fusion.96, f32[2,4,128,1584]{2,3,1,0:T(8,128)} %fusion.104, f32[2,4,128,1584]{2,3,1,0:T(8,128)} %fusion.112, f32[2,4,128,1584]{2,3,1,0:T(8,128)} %fusion.120, f32[2,4,128,1584]{2,3,1,0:T(8,128)} %fusion.128, f32[2,4,128,1584]{2,3,1,0:T(8,128)} %fusion.144, ...), kind=kOutput, calls=%fused_computation.2 | convolution fusion | flops 128139264 | bytes 52111360 | tf_op jit(solution)/shard_map/qi,fsin->fsqn/dot_general | solution.py:37
  296.4 18.0 %add_bitcast_fusion.3 = f32[2,4,1584,128]{3,2,1,0:T(8,128)} fusion(f32[2,4,128,1584]{2,3,1,0:T(8,128)} %fusion.98, f32[2,4,128,1584]{2,3,1,0:T(8,128)} %fusion.106, f32[2,4,128,1584]{2,3,1,0:T(8,128)} %fusion.114, f32[2,4,128,1584]{2,3,1,0:T(8,128)} %fusion.122, f32[2,4,128,1584]{2,3,1,0:T(8,128)} %fusion.130, f32[2,4,128,1584]{2,3,1,0:T(8,128)} %fusion.146, ...), kind=kOutput, calls=%fused_computation.3 | convolution fusion | flops 128139264 | bytes 52111360 | tf_op jit(solution)/shard_map/qi,fsin->fsqn/dot_general | solution.py:37
  314.5 10.8 %add_convert_fusion = (bf16[1,4,1584,128]{3,2,1,0:T(8,128)(2,1)S(1)}, bf16[1,4,1584,128]{3,2,1,0:T(8,128)(2,1)S(1)}, bf16[1,4,1584,128]{3,2,1,0:T(8,128)(2,1)S(1...) fusion(f32[2,4,1584,128]{3,2,1,0:T(8,128)} %add_bitcast_fusion,, ...), kind=kLoop, calls=%fused_computation.55 | loop fusion | flops 32440320 | bytes 38941056 | tf_op jit(solution)/shard_map/convert
  348.4 62.9 %all_to_all.24 = f32[2,128,36,128]{3,0,2,1:T(2,128)S(1)} all-to-all(f32[2,128,36,128]{3,0,2,1:T(2,128)S(1)} %copy.174), channel_id=1, replica_groups=mesh['mode'=8,'col'=16] {'mode','col'}, dimensions={1} | all-to-all | bytes 9437184 | tf_op jit(solution)/shard_map/all_to_all | solution.py:84
  416.4 6.3 %mul.170 = f32[2,36,64,256]{3,2,1,0:T(8,128)} reshape(f32[2,1,36,128,128]{4,3,2,0,1:T(8,128)} %copy.175) | data formatting | bytes 9437184 | tf_op jit(solution)/shard_map/mul | solution.py:86
  422.6 4.7 add.234
  435.5 4.0 collective-permute-done.1
  441.7 12.6 %fusion.4 = f32[2,36,64,256]{3,2,1,0:T(8,128)S(1)} fusion(f32[2,36,64,256]{3,2,1,0:T(8,128)} %copy-done, f32[2,36,64,1]{3,2,1,0:T(8,128)} %copy.179, f32[2,36,64,1]{3,2,1,0:T(8,128)S(1)} %copy.177, f32[2]{0:T(128)S(1)} %copy-done.8, f32[2]{0:T(128)S(1)} %copy-done.7), kind=kLoop, calls=%fused_computation.21 | loop fusion | flops 9437184 | bytes 9474064 | tf_op jit(solution)/shard_map/div | solution.py:98
  462.2 4.3 collective-permute-done.3
  468.6 11.7 %fusion.9 = f32[2,36,64,256]{3,2,1,0:T(8,128)S(1)} fusion(f32[2,36,64,256]{3,2,1,0:T(8,128)} %copy-done, f32[2,36,64,256]{3,2,1,0:T(8,128)} %copy-done.1, f32[2,36,64,1]{3,2,1,0:T(8,128)} %copy.183, f32[2,36,64,1]{3,2,1,0:T(8,128)S(1)} %copy.181, f32[2]{0:T(128)S(1)} %copy-done.8, f32[2]{0:T(128)S(1)} %copy-done.7), kind=kLoop, calls=%fused_computation.26 | loop fusion | flops 9437184 | bytes 14192656 | tf_op jit(solution)/shard_map/div | solution.py:98
  488.2 4.0 collective-permute-done.5
  494.4 11.7 %fusion.14 = f32[2,36,64,256]{3,2,1,0:T(8,128)S(1)} fusion(f32[2,36,64,256]{3,2,1,0:T(8,128)} %copy-done, f32[2,36,64,256]{3,2,1,0:T(8,128)} %copy-done.3, f32[2,36,64,1]{3,2,1,0:T(8,128)} %copy.187, f32[2,36,64,1]{3,2,1,0:T(8,128)S(1)} %copy.185, f32[2]{0:T(128)S(1)} %copy-done.8, f32[2]{0:T(128)S(1)} %copy-done.7), kind=kLoop, calls=%fused_computation.31 | loop fusion | flops 9437184 | bytes 14192656 | tf_op jit(solution)/shard_map/div | solution.py:98
  514.1 4.3 collective-permute-done.7
  520.5 13.1 %fusion.19 = f32[2,36,64,256]{3,2,1,0:T(8,128)} fusion(f32[2,36,64,256]{3,2,1,0:T(8,128)} %copy-done, f32[2,36,64,256]{3,2,1,0:T(8,128)} %copy-done.2, f32[2,36,64,1]{3,2,1,0:T(8,128)} %copy.191, f32[2,36,64,1]{3,2,1,0:T(8,128)S(1)} %copy.189, f32[2]{0:T(128)S(1)} %copy-done.8, f32[2]{0:T(128)S(1)} %copy-done.7), kind=kLoop, calls=%fused_computation.36 | loop fusion | flops 9437184 | bytes 14192656 | tf_op jit(solution)/shard_map/div | solution.py:98
  (113 shorter events, 139.7 us)
Async XLA Ops:
  40.7 11.2 %copy-start.6 = (f32[1584]{0:T(1024)S(1)}, f32[1584]{0:T(1024)}, u32[]{:S(2)}) copy-start(f32[1584]{0:T(1024)} %param.9) | copy-start | bytes 19012
  40.7 11.2 %copy-start.9 = (f32[1584]{0:T(1024)S(1)}, f32[1584]{0:T(1024)}, u32[]{:S(2)}) copy-start(f32[1584]{0:T(1024)} %param.10) | copy-start | bytes 19012
  40.7 44.4 %all-to-all-start = ((bf16[128,2,4608]{2,1,0:T(2,128)(2,1)}), bf16[128,2,4608]{2,1,0:T(2,128)(2,1)S(1)}, u32[]{:S(2)}, u32[]{:S(2)}) async-start(bf16[128,2,4608]{2,1,0:T(2,128)(2,1)} %reshape.44), calls=%async_computation | async-start | bytes 4718592 | tf_op jit(solution)/shard_map/all_to_all | solution.py:79
  122.6 1.5 copy-start.4
  242.1 18.2 %copy-start.5 = (bf16[2,1,4,36,128]{4,2,1,0,3:T(4,128)(2,1)S(1)}, bf16[2,1,4,36,128]{4,2,1,0,3:T(4,128)(2,1)}, u32[]{:S(2)}) copy-start(bf16[2,1,4,36,128]{4,2,1,0,3:T(4,128)(2,1)} %get-tuple-element.52) | copy-start | bytes 221188
  314.5 10.8 %copy-start.10 = (bf16[288,1584]{1,0:T(8,128)(2,1)S(1)}, bf16[288,1584]{1,0:T(8,128)(2,1)}, u32[]{:S(2)}) copy-start(bf16[288,1584]{1,0:T(8,128)(2,1)} %param.8) | copy-start | bytes 2737156
  427.3 2.9 copy-start
  432.7 2.0 collective-permute-start
  433.1 8.6 %copy-start.7 = (f32[2]{0:T(128)S(1)}, f32[2]{0:T(128)}, u32[]{:S(2)}) copy-start(f32[2]{0:T(128)} %constant.12.clone) | copy-start | bytes 28
  433.1 8.6 %copy-start.8 = (f32[2]{0:T(128)S(1)}, f32[2]{0:T(128)}, u32[]{:S(2)}) copy-start(f32[2]{0:T(128)} %constant.24) | copy-start | bytes 28
  433.9 5.6 %collective-permute-start.1 = (f32[2,36,64,1]{2,1,3,0:T(8,128)S(1)}, f32[2,36,64,1]{2,1,3,0:T(8,128)S(1)}, u32[]{:S(2)}, u32[]{:S(2)}) collective-permute-start(f32[2,36,64,1]{2,1,3,0:T(8,128)S(1)} %copy.178), channel_id=1, source_target_pairs={{0,1},{1,2},{2,3},{3,4},{4,5},{5,6},{6,7},{7,8},{8,9},{9,10},{10,1... | collective-permute-start | bytes 55304 | tf_op jit(solution)/shard_map/ppermute | solution.py:22
  454.3 2.9 copy-start.1
  459.7 1.7 collective-permute-start.2
  460.6 5.8 %collective-permute-start.3 = (f32[2,36,64,1]{2,1,3,0:T(8,128)S(1)}, f32[2,36,64,1]{2,1,3,0:T(8,128)S(1)}, u32[]{:S(2)}, u32[]{:S(2)}) collective-permute-start(f32[2,36,64,1]{2,1,3,0:T(8,128)S(1)} %copy.182), channel_id=1, source_target_pairs={{0,1},{1,2},{2,3},{3,4},{4,5},{5,6},{6,7},{7,8},{8,9},{9,10},{10,1... | collective-permute-start | bytes 55304 | tf_op jit(solution)/shard_map/ppermute | solution.py:22
  480.4 2.9 copy-start.3
  485.7 1.7 collective-permute-start.4
  486.7 5.6 %collective-permute-start.5 = (f32[2,36,64,1]{2,1,3,0:T(8,128)S(1)}, f32[2,36,64,1]{2,1,3,0:T(8,128)S(1)}, u32[]{:S(2)}, u32[]{:S(2)}) collective-permute-start(f32[2,36,64,1]{2,1,3,0:T(8,128)S(1)} %copy.186), channel_id=1, source_target_pairs={{0,1},{1,2},{2,3},{3,4},{4,5},{5,6},{6,7},{7,8},{8,9},{9,10},{10,1... | collective-permute-start | bytes 55304 | tf_op jit(solution)/shard_map/ppermute | solution.py:22
  506.2 2.9 copy-start.2
  511.5 1.7 collective-permute-start.6
  512.5 5.9 %collective-permute-start.7 = (f32[2,36,64,1]{2,1,3,0:T(8,128)S(1)}, f32[2,36,64,1]{2,1,3,0:T(8,128)S(1)}, u32[]{:S(2)}, u32[]{:S(2)}) collective-permute-start(f32[2,36,64,1]{2,1,3,0:T(8,128)S(1)} %copy.190), channel_id=1, source_target_pairs={{0,1},{1,2},{2,3},{3,4},{4,5},{5,6},{6,7},{7,8},{8,9},{9,10},{10,1... | collective-permute-start | bytes 55304 | tf_op jit(solution)/shard_map/ppermute | solution.py:22
where the time goes:
time: 541 us; the launch traced here: 534 us
  matrix products  208 us (38%)
  local copies, waits for them, and re-layouts  127 us (23%)
  other arithmetic  69.8 us (13%)
  blocking collectives  62.9 us (12%)
  waiting for transfers between devices  50.6 us (9%)
  starting transfers between devices  14.1 us (3%)
    dot_general x28, matrix products, react_sources(): jnp.einsum('qi,fsin->fsqn', eval_parts[group_index], block[:, group_index...  175 us
    all_to_all x1, blocking collectives, body(): lax.all_to_all(projected, ('mode', 'col'), split_axis=1, concat_axis=3, t...  62.9 us
    unnamed x24, local copies, waits for them, and re-layouts  53.8 us
    div x4, other arithmetic, body(): iterate = (right_side + weights * neighbours) / (1.0 + 4.0 * weights)  49.2 us
    all_to_all x1, waiting for transfers between devices, body(): lax.all_to_all(rounded, ('mode', 'col'), split_axis=3, concat_axis=1, til...  33.2 us
    slice x8, local copies, waits for them, and re-layouts, padded_2(): head = lax.slice_in_dim(cells, 0, width, axis=dim)  20.9 us
    dot_general x32, matrix products, react_sources(): jnp.einsum('iq,fsqn->fsin', proj_parts[group_index], reacted, preferred_e...  17.9 us
    ppermute x4, waiting for transfers between devices, padded_2(): lax.ppermute(tail, axis, [(i, (i + 1) % count) for i in range(count)])  16.5 us
  transfers between devices with their start and end apart: 9, of which 7 were waited for; matrix products, arithmetic and copies ran while one was open for 1% of the time, Pallas kernels for 0%

commit v1 on v0

v1 whole, which is shorter than its diff:
```python
import jax
import jax.numpy as jnp
from jax import lax
from jax.experimental import pallas as pl
from jax.experimental.pallas import tpu as pltpu
from jax.sharding import PartitionSpec as P

MESH = pl.DeviceIdType.MESH
F32, BF16 = jnp.float32, jnp.bfloat16

SWEEPS = 4
TIME_STEP = 0.5
DIFFUSION = (1.0, 0.5)

MODES, POINTS = 288, 1584
PARTS = 8
LOCAL = 36
ROWS, COLS = 64, 256
CHUNKS = 4
TILES = 9
MESSAGE = 144
DEPTH = 384
PADDED = 1664
BLOCK = 528
OUT_ROWS = 320
GROUPS = ((0, 3), (3, 6), (6, 9))
PARTNERS = ((0, 1), (1, 0), (3, 0), (2, 0), (1, 1), (3, 1), (2, 1))


def iota(shape, dim):
    return lax.broadcasted_iota(jnp.int32, shape, dim)


def kernel(
    fields, evaluate, project, rates, out,
    fv, ft, ita, itb, ev, pj, weights, proj, rate_b,
    snd, rcv, reacted, bsnd, brcv, hsnd, hrcv,
    in_sem, table_sem, out_sem, own_sem, fs_sem, fr_sem, bown_sem, bs_sem, br_sem, hs_sem, hr_sem,
):
    me, col = lax.axis_index("mode"), lax.axis_index("col")
    cols = lax.axis_size("col")
    right, left = (col + 1) % cols, (col + cols - 1) % cols
    partners = [((me // 2 + dy) % 4) * 2 + (me % 2 + dx) % 2 for dy, dx in PARTNERS]

    barrier = pltpu.get_barrier_semaphore()
    for part in partners:
        pl.semaphore_signal(barrier, inc=1, device_id=(part, col), device_id_type=MESH)
    for side in (right, left):
        pl.semaphore_signal(barrier, inc=1, device_id=(me, side), device_id_type=MESH)

    planes = fv.reshape(2, 2 * LOCAL, ROWS, 128)

    def load(chunk, half):
        rows = pl.ds(16 * chunk, 16)
        return pltpu.make_async_copy(
            fields.at[:, rows, pl.ds(128 * half, 128)], planes.at[half, :, rows, :], in_sem.at[chunk, half]
        )

    for chunk in range(CHUNKS):
        for half in range(2):
            load(chunk, half).start()
    tables = [
        pltpu.make_async_copy(evaluate, ev, table_sem.at[0]),
        pltpu.make_async_copy(project, pj, table_sem.at[1]),
    ]
    for table in tables:
        table.start()

    def prepare(chunk):
        def one(dest, carry):
            row = 16 * chunk + 2 * dest
            values = []
            for j in range(2):
                values.append([])
                for g in range(TILES):
                    rows = pl.ds(8 * g * ROWS + row + j, 8, stride=ROWS)
                    values[j].append(jnp.concatenate([fv[0, rows, :], fv[1, rows, :]], axis=1))
                for g in range(TILES):
                    ft[g, row + j + 1, :, :COLS] = values[j][g]
            for j in range(2):
                for k, g in enumerate((0, 2, 5, 7)):
                    pair = jnp.concatenate([values[j][g], values[j][g + 1]], axis=0)
                    snd[dest, chunk, 64 * j + 16 * k : 64 * j + 16 * k + 16, :] = pair.astype(BF16)
            pair = jnp.concatenate([values[0][4], values[1][4]], axis=0)
            snd[dest, chunk, 128:144, :] = pair.astype(BF16)
            return carry

        lax.fori_loop(0, PARTS, one, 0)

    def forward(chunk, k):
        part = partners[k]
        return pltpu.make_async_remote_copy(
            src_ref=snd.at[part, chunk], dst_ref=rcv.at[chunk, me],
            send_sem=fs_sem.at[chunk, k], recv_sem=fr_sem.at[chunk, me],
            device_id=(part, col), device_id_type=MESH,
        )

    def forward_in(chunk, k):
        part = partners[k]
        return pltpu.make_async_remote_copy(
            src_ref=snd.at[part, chunk], dst_ref=rcv.at[chunk, part],
            send_sem=fs_sem.at[chunk, k], recv_sem=fr_sem.at[chunk, part],
            device_id=(part, col), device_id_type=MESH,
        )

    def own(chunk):
        return pltpu.make_async_copy(snd.at[me, chunk], rcv.at[chunk, me], own_sem.at[chunk])

    for half in range(2):
        load(0, half).wait()
    prepare(0)
    pl.semaphore_wait(barrier, len(PARTNERS) + 2)
    for chunk in range(CHUNKS):
        if chunk > 0:
            for half in range(2):
                load(chunk, half).wait()
            prepare(chunk)
        for k in range(len(PARTNERS)):
            forward(chunk, k).start()
        own(chunk).start()

    for g in range(TILES):
        ft[g, 0, :, :] = jnp.zeros((8, DEPTH), F32)
        ft[g, ROWS + 1, :, :] = jnp.zeros((8, DEPTH), F32)
    for ref in (ita, itb):
        ref[0, :, :] = jnp.zeros((8, DEPTH), F32)
        ref[ROWS + 1, :, :] = jnp.zeros((8, DEPTH), F32)
    for table in tables:
        table.wait()
    mode = iota((MODES, DEPTH), 0)
    slot = iota((MODES, DEPTH), 1)
    mixed = slot - 256
    for f in range(2):
        main_mode = LOCAL * (slot >> 5) + (slot & 31) + 4 * f
        place = mixed & 7
        mix_mode = LOCAL * (mixed >> 4) + (place - 4 if f else place + 32)
        for j in range(2):
            mine = (((mixed >> 3) & 1) == j) & ((place >= 4) if f else (place < 4))
            want = jnp.where(slot < 256, main_mode, jnp.where(mine, mix_mode, -1))
            onehot = jnp.where(want == mode, 1.0, 0.0).astype(BF16)
            weights[2 * f + j] = jnp.dot(ev[...], onehot, preferred_element_type=F32).astype(BF16)
    mode = iota((OUT_ROWS, MODES), 1)
    slot = iota((OUT_ROWS, MODES), 0)
    mixed = slot - 256
    for f in range(2):
        main_mode = LOCAL * (slot >> 5) + (slot & 31) + 4 * f
        place = mixed & 7
        mix_mode = LOCAL * (mixed >> 3) + (place - 4 if f else place + 32)
        mine = (place >= 4) if f else (place < 4)
        want = jnp.where(slot < 256, main_mode, jnp.where(mine, mix_mode, -1))
        onehot = jnp.where(want == mode, 1.0, 0.0).astype(BF16)
        proj[f, :, 1536:] = jnp.zeros((OUT_ROWS, 128), BF16)
        proj[f, :, :POINTS] = jnp.dot(onehot, pj[...], preferred_element_type=F32).astype(BF16)
        reacted[f, POINTS:, :] = jnp.zeros((PADDED - POINTS, 2 * COLS), BF16)
    eye = iota((128, 128), 0) == iota((128, 128), 1)
    for q in range(0, POINTS, 128):
        count = min(128, POINTS - q)
        for f in range(2):
            spread = jnp.broadcast_to(rates[f : f + 1, q : q + 128], (128, 128))
            column = jnp.sum(jnp.where(eye, spread, 0.0), axis=1, keepdims=True)
            rate_b[f, q : q + count, :] = jnp.broadcast_to(column[:count], (count, 128))

    def react(chunk):
        for k in range(len(PARTNERS)):
            forward_in(chunk, k).wait_recv()
        own(chunk).wait()

        def block(b, carry):
            rows = pl.ds(pl.multiple_of(b * BLOCK, 16), BLOCK)
            feed = jnp.tile(rate_b[0, rows, :], (1, 2))
            loss = jnp.tile(rate_b[1, rows, :], (1, 2))
            for j in range(2):
                mix = rcv[chunk, :, 128:144, :].reshape(128, COLS)
                ub = jnp.concatenate([rcv[chunk, :, 64 * j : 64 * j + 32, :].reshape(256, COLS), mix], axis=0)
                vb = jnp.concatenate([rcv[chunk, :, 64 * j + 32 : 64 * j + 64, :].reshape(256, COLS), mix], axis=0)
                u = jnp.dot(weights[j, rows, :], ub, preferred_element_type=F32)
                v = jnp.dot(weights[2 + j, rows, :], vb, preferred_element_type=F32)
                squared = u * v * v
                lanes = slice(COLS * j, COLS * j + COLS)
                reacted[0, rows, lanes] = (feed * (1.0 - u) - squared).astype(BF16)
                reacted[1, rows, lanes] = (squared - loss * v).astype(BF16)
            return carry

        lax.fori_loop(0, POINTS // BLOCK, block, 0)

    def project_back(chunk):
        mix = None
        for f in range(2):
            total = jnp.dot(proj[f], reacted[f], preferred_element_type=F32)
            main = jnp.stack(
                [total[:256, :COLS].reshape(32, 8, COLS), total[:256, COLS:].reshape(32, 8, COLS)], axis=1
            ).astype(BF16)
            bsnd[:, 5 * f : 5 * f + 4, chunk] = main.reshape(PARTS, 4, 16, COLS)
            mix = total[256:] if f == 0 else mix + total[256:]
        mix = jnp.stack([mix[:, :COLS].reshape(8, 8, COLS), mix[:, COLS:].reshape(8, 8, COLS)], axis=1)
        bsnd[:, 4, chunk] = mix.astype(BF16).reshape(PARTS, 16, COLS)

    def part_of(item, row):
        first, last = GROUPS[max(0, item - 3)]
        if item < CHUNKS:
            return row[0].at[row[1], first:last, item]
        return row[0].at[row[1], first:last]

    def backward(item, k, incoming=False):
        part = partners[k]
        slot = part if incoming else me
        return pltpu.make_async_remote_copy(
            src_ref=part_of(item, (bsnd, part)), dst_ref=part_of(item, (brcv, slot)),
            send_sem=bs_sem.at[item, k], recv_sem=br_sem.at[item, slot],
            device_id=(part, col), device_id_type=MESH,
        )

    def back_own(item):
        return pltpu.make_async_copy(part_of(item, (bsnd, me)), part_of(item, (brcv, me)), bown_sem.at[item])

    def send_back(item):
        for k in range(len(PARTNERS)):
            backward(item, k).start()
        back_own(item).start()

    items = CHUNKS + len(GROUPS) - 1
    for chunk in range(CHUNKS):
        react(chunk)
        project_back(chunk)
        send_back(chunk)
    for item in range(CHUNKS, items):
        send_back(item)

    lane = iota((8, 128), 1)

    def gather(index):
        first, last = GROUPS[index]
        for item in range(CHUNKS) if index == 0 else (CHUNKS + index - 1,):
            for k in range(len(PARTNERS)):
                backward(item, k, True).wait_recv()
            back_own(item).wait()

        def tile(g, carry):
            def rows16(c, carry):
                packed = jnp.zeros((8, 128), F32)
                for s in range(PARTS):
                    pair = brcv[s, g, c].astype(F32)
                    for j in range(2):
                        row = 16 * c + 2 * s + j + 1
                        value = ft[g, row, :, :COLS] + TIME_STEP * pair[8 * j : 8 * j + 8]
                        ft[g, row, :, :COLS] = value
                        edge = jnp.where(lane < 64, value[:, :128], value[:, 128:])
                        at = 2 * s + j
                        packed = jnp.where((lane >> 3) == at, pltpu.roll(edge, (8 * at + 4) % 128, 1), packed)
                hsnd[g, c] = packed
                return carry

            return lax.fori_loop(0, CHUNKS, rows16, carry)

        lax.fori_loop(first, last, tile, 0)

    def halo(index, side, incoming=False):
        first, last = GROUPS[index]
        there = 1 - side if incoming else side
        return pltpu.make_async_remote_copy(
            src_ref=hsnd.at[first:last], dst_ref=hrcv.at[there, first:last],
            send_sem=hs_sem.at[index, side], recv_sem=hr_sem.at[index, there],
            device_id=(me, left if side else right), device_id_type=MESH,
        )

    def sweeps(index):
        first, last = GROUPS[index]
        for side in range(2):
            halo(index, side, True).wait_recv()

        def tile(g, carry):
            pair = 8 * g + iota((8, DEPTH), 0)
            weight = jnp.where(pair < LOCAL, DIFFUSION[0], DIFFUSION[1])
            keep = jnp.broadcast_to((1.0 / (1.0 + 4.0 * weight))[None], (8, 8, DEPTH)).reshape(64, DEPTH)
            near = jnp.broadcast_to((weight / (1.0 + 4.0 * weight))[None], (8, 8, DEPTH)).reshape(64, DEPTH)

            def widen(c, carry):
                both = jnp.where((lane & 7) < 4, hrcv[0, g, c], hrcv[1, g, c])
                for at in range(16):
                    ft[g, 16 * c + at + 1, :, COLS:] = pltpu.roll(both, (124 - 8 * at) % 128, 1)
                return carry

            lax.fori_loop(0, CHUNKS, widen, 0)

            def sweep(source, store):
                def rows8(b, carry):
                    start = 8 * b
                    window = source(pl.ds(start, 10))
                    middle = window[1:9].reshape(64, DEPTH)
                    total = (window[0:8] + window[2:10]).reshape(64, DEPTH)
                    total = total + (pltpu.roll(middle, 1, 1) + pltpu.roll(middle, DEPTH - 1, 1))
                    base = ft[g, pl.ds(start + 1, 8)].reshape(64, DEPTH)
                    store(start, (keep * base + near * total).reshape(8, 8, DEPTH))
                    return carry

                lax.fori_loop(0, ROWS // 8, rows8, 0)

            def into(ref):
                def store(start, value):
                    ref[pl.ds(start + 1, 8)] = value

                return store

            def last_store(start, value):
                for i in range(8):
                    rows = pl.ds(8 * g * ROWS + start + i, 8, stride=ROWS)
                    fv[0, rows, :] = value[i, :, :128]
                    fv[1, rows, :] = value[i, :, 128:COLS]

            sweep(lambda rows: ft[g, rows], into(ita))
            sweep(lambda rows: ita[rows], into(itb))
            sweep(lambda rows: itb[rows], into(ita))
            sweep(lambda rows: ita[rows], last_store)
            return carry

        lax.fori_loop(first, last, tile, 0)

    def write(index, half):
        first, last = GROUPS[index]
        rows = pl.ds(8 * first, 8 * (last - first))
        return pltpu.make_async_copy(
            planes.at[half, rows], out.at[rows, :, pl.ds(128 * half, 128)], out_sem.at[index, half]
        )

    count = len(GROUPS)
    for index in range(count + 1):
        if index < count:
            gather(index)
            for side in range(2):
                halo(index, side).start()
        if index > 0:
            sweeps(index - 1)
            for half in range(2):
                write(index - 1, half).start()

    for chunk in range(CHUNKS):
        for k in range(len(PARTNERS)):
            forward(chunk, k).wait_send()
    for item in range(items):
        for k in range(len(PARTNERS)):
            backward(item, k).wait_send()
    for index in range(count):
        for side in range(2):
            halo(index, side).wait_send()
            write(index, side).wait()


def body(fields, evaluate, project, feed, kill):
    rates = jnp.pad(jnp.stack([feed, feed + kill]), ((0, 0), (0, PADDED - POINTS)))
    items = CHUNKS + len(GROUPS) - 1
    partners = len(PARTNERS)
    anywhere = pl.BlockSpec(memory_space=pl.ANY)
    dma = pltpu.SemaphoreType.DMA
    stepped = pl.pallas_call(
        kernel,
        out_shape=jax.ShapeDtypeStruct((2 * LOCAL, ROWS, COLS), F32),
        in_specs=[anywhere, anywhere, anywhere, pl.BlockSpec(memory_space=pltpu.VMEM)],
        out_specs=anywhere,
        scratch_shapes=[
            pltpu.VMEM((2, 2 * LOCAL * ROWS, 128), F32),
            pltpu.VMEM((TILES, ROWS + 2, 8, DEPTH), F32),
            pltpu.VMEM((ROWS + 2, 8, DEPTH), F32),
            pltpu.VMEM((ROWS + 2, 8, DEPTH), F32),
            pltpu.VMEM((POINTS, MODES), BF16),
            pltpu.VMEM((MODES, POINTS), BF16),
            pltpu.VMEM((4, POINTS, DEPTH), BF16),
            pltpu.VMEM((2, OUT_ROWS, PADDED), BF16),
            pltpu.VMEM((2, POINTS, 128), F32),
            pltpu.VMEM((PARTS, CHUNKS, MESSAGE, COLS), BF16),
            pltpu.VMEM((CHUNKS, PARTS, MESSAGE, COLS), BF16),
            pltpu.VMEM((2, PADDED, 2 * COLS), BF16),
            pltpu.VMEM((PARTS, TILES, CHUNKS, 16, COLS), BF16),
            pltpu.VMEM((PARTS, TILES, CHUNKS, 16, COLS), BF16),
            pltpu.VMEM((TILES, CHUNKS, 8, 128), F32),
            pltpu.VMEM((2, TILES, CHUNKS, 8, 128), F32),
            dma((CHUNKS, 2)),
            dma((2,)),
            dma((len(GROUPS), 2)),
            dma((CHUNKS,)),
            dma((CHUNKS, partners)),
            dma((CHUNKS, PARTS)),
            dma((items,)),
            dma((items, partners)),
            dma((items, PARTS)),
            dma((len(GROUPS), 2)),
            dma((len(GROUPS), 2)),
        ],
        compiler_params=pltpu.CompilerParams(
            collective_id=0, has_side_effects=True, vmem_limit_bytes=60 * 2**20
        ),
        cost_estimate=pl.CostEstimate(
            flops=8 * 2 * LOCAL * ROWS * COLS * POINTS // 2, bytes_accessed=12 * 2**20, transcendentals=0
        ),
    )(fields.reshape(2 * LOCAL, ROWS, COLS), evaluate, project, rates)
    return stepped.reshape(2, LOCAL, ROWS, COLS)


def solution(mesh):
    in_specs = (P(None, "mode", None, "col"), P(), P(), P(), P())
    out_specs = P(None, "mode", None, "col")
    return jax.shard_map(body, mesh=mesh, in_specs=in_specs, out_specs=out_specs, check_vma=False)
```

time: 541 us -> 115 us (0.21); the launches traced: 534 us -> 115 us
  matrix products: 208 us -> 0 us
  local copies, waits for them, and re-layouts: 127 us -> 8.21 us
  Pallas kernels: 0 us -> 105 us
  other arithmetic: 69.8 us -> 1.33 us
  blocking collectives: 62.9 us -> 0 us
  waiting for transfers between devices: 50.6 us -> 0 us
  starting transfers between devices: 14.1 us -> 0 us
    dot_general x64 -> x0, matrix products: 208 us -> none  [the longest x28 175 us: react_sources(): jnp.einsum('qi,fsin->fsqn', eval_parts[group_index], block[:, group_index...]
    pallas_call x0 -> x1, Pallas kernels: none -> 105 us  [body(): pl.pallas_call(kernel, out_shape=jax.ShapeDtypeStruct((2 * LOCAL, ROWS, C...]
    all_to_all x1 -> x0, blocking collectives: 62.9 us -> none  [body(): lax.all_to_all(projected, ('mode', 'col'), split_axis=1, concat_axis=3, t...]
    div x4 -> x0, other arithmetic: 49.2 us -> none  [body(): iterate = (right_side + weights * neighbours) / (1.0 + 4.0 * weights)]
    unnamed x24 -> x2, local copies, waits for them, and re-layouts: 53.8 us -> 7.5 us
    all_to_all x1 -> x0, waiting for transfers between devices: 33.2 us -> none  [body(): lax.all_to_all(rounded, ('mode', 'col'), split_axis=3, concat_axis=1, til...]
    slice x14 -> x0, local copies, waits for them, and re-layouts: 25.7 us -> none  [the longest x8 20.9 us: padded_2(): head = lax.slice_in_dim(cells, 0, width, axis=dim)]
    ppermute x8 -> x0, waiting for transfers between devices: 17.4 us -> none  [the longest x4 16.5 us: padded_2(): lax.ppermute(tail, axis, [(i, (i + 1) % count) for i in range(count)])]
  transfers between devices with their start and end apart: 9 -> 0, of which waited for: 7 -> 0; matrix products, arithmetic and copies ran while one was open for 1% -> 0% of each run, Pallas kernels for 0% -> 0%
where the time goes in v1:
time: 115 us
  Pallas kernels  105 us (91%)
  local copies, waits for them, and re-layouts  8.21 us (7%)
  other arithmetic  1.33 us (1%)
    pallas_call x1, Pallas kernels, body(): pl.pallas_call(kernel, out_shape=jax.ShapeDtypeStruct((2 * LOCAL, ROWS, C...  105 us
    unnamed x2, local copies, waits for them, and re-layouts  7.5 us

profile of v1, /device:TPU:0, one launch (start us, length us, event | category | flops | bytes accessed | tf_op | source)
XLA Modules:
  0.0 114.5 jit_solution(6861137212602856937)
XLA Ops:
  0.0 0.7 stack.9
  0.7 0.7 add.5
  1.4 0.6 select_maximum_fusion.rates
  2.0 2.4 %copy.6.evaluate = bf16[1584,288]{1,0:T(8,128)(2,1)} copy(bf16[1584,288]{0,1:T(8,128)(2,1)} %param.6) | data formatting | bytes 1824768 | tf_op args[1]
  4.4 105.0 %shard_map.55 = f32[72,64,256]{2,1,0:T(8,128)} custom-call(f32[72,64,256]{2,1,0:T(8,128)} %bitcast.3, bf16[1584,288]{1,0:T(8,128)(2,1)} %copy.6.evaluate, bf16[288,1584]{1,0:T(8,128)(2,1)} %project.1, f32[2,1664]{1,0:T(2,128)} %select_maximum_fusion.rates), custom_call_target="tpu_custom_call" | custom-call | flops 7474249728 | bytes 12582912 | tf_op jit(solution)/shard_map/pallas_call | solution.py:354
  109.4 5.1 %copy.8 = f32[2,36,64,256]{3,2,1,0:T(8,128)} copy(f32[2,36,64,256]{3,2,1,0:T(8,128)} %bitcast.2) | data formatting | bytes 9437184
  (1 shorter events, 0.0 us)

commit v2 on v1

--- a/solution.py
+++ b/solution.py
@@ -8,7 +8,7 @@
 MESH = pl.DeviceIdType.MESH
 F32, BF16 = jnp.float32, jnp.bfloat16
 
-SWEEPS = 4
+VMEM_LIMIT = 58 * 2**20
 TIME_STEP = 0.5
 DIFFUSION = (1.0, 0.5)
 
@@ -23,7 +23,7 @@
 PADDED = 1664
 BLOCK = 528
 OUT_ROWS = 320
-GROUPS = ((0, 3), (3, 6), (6, 9))
+GROUPS = ((0, 2), (2, 4), (4, 6), (6, 8), (8, 9))
 PARTNERS = ((0, 1), (1, 0), (3, 0), (2, 0), (1, 1), (3, 1), (2, 1))
 
 
@@ -32,7 +32,7 @@
 
 
 def kernel(
-    fields, evaluate, project, rates, out,
+    fields, evaluate, project, feed, kill, out,
     fv, ft, ita, itb, ev, pj, weights, proj, rate_b,
     snd, rcv, reacted, bsnd, brcv, hsnd, hrcv,
     in_sem, table_sem, out_sem, own_sem, fs_sem, fr_sem, bown_sem, bs_sem, br_sem, hs_sem, hr_sem,
@@ -138,7 +138,9 @@
             mine = (((mixed >> 3) & 1) == j) & ((place >= 4) if f else (place < 4))
             want = jnp.where(slot < 256, main_mode, jnp.where(mine, mix_mode, -1))
             onehot = jnp.where(want == mode, 1.0, 0.0).astype(BF16)
-            weights[2 * f + j] = jnp.dot(ev[...], onehot, preferred_element_type=F32).astype(BF16)
+            weights[2 * f + j] = lax.dot_general(
+                ev[...], onehot, (((0,), (0,)), ((), ())), preferred_element_type=F32
+            ).astype(BF16)
     mode = iota((OUT_ROWS, MODES), 1)
     slot = iota((OUT_ROWS, MODES), 0)
     mixed = slot - 256
@@ -153,12 +155,11 @@
         proj[f, :, :POINTS] = jnp.dot(onehot, pj[...], preferred_element_type=F32).astype(BF16)
         reacted[f, POINTS:, :] = jnp.zeros((PADDED - POINTS, 2 * COLS), BF16)
     eye = iota((128, 128), 0) == iota((128, 128), 1)
-    for q in range(0, POINTS, 128):
-        count = min(128, POINTS - q)
-        for f in range(2):
-            spread = jnp.broadcast_to(rates[f : f + 1, q : q + 128], (128, 128))
-            column = jnp.sum(jnp.where(eye, spread, 0.0), axis=1, keepdims=True)
-            rate_b[f, q : q + count, :] = jnp.broadcast_to(column[:count], (count, 128))
+    for q in (*range(0, POINTS - 128, 128), POINTS - 128):
+        supply = feed[q : q + 128].reshape(1, 128)
+        for f, rate in enumerate((supply, supply + kill[q : q + 128].reshape(1, 128))):
+            column = jnp.sum(jnp.where(eye, jnp.broadcast_to(rate, (128, 128)), 0.0), axis=1, keepdims=True)
+            rate_b[f, q : q + 128, :] = jnp.broadcast_to(column, (128, 128))
 
     def react(chunk):
         for k in range(len(PARTNERS)):
@@ -223,8 +224,7 @@
         react(chunk)
         project_back(chunk)
         send_back(chunk)
-    for item in range(CHUNKS, items):
-        send_back(item)
+    send_back(CHUNKS)
 
     lane = iota((8, 128), 1)
 
@@ -234,6 +234,8 @@
             for k in range(len(PARTNERS)):
                 backward(item, k, True).wait_recv()
             back_own(item).wait()
+        if index + 2 < len(GROUPS):
+            send_back(CHUNKS + index + 1)
 
         def tile(g, carry):
             def rows16(c, carry):
@@ -269,10 +271,10 @@
             halo(index, side, True).wait_recv()
 
         def tile(g, carry):
-            pair = 8 * g + iota((8, DEPTH), 0)
+            pair = 8 * g + iota((8, 128), 0)
             weight = jnp.where(pair < LOCAL, DIFFUSION[0], DIFFUSION[1])
-            keep = jnp.broadcast_to((1.0 / (1.0 + 4.0 * weight))[None], (8, 8, DEPTH)).reshape(64, DEPTH)
-            near = jnp.broadcast_to((weight / (1.0 + 4.0 * weight))[None], (8, 8, DEPTH)).reshape(64, DEPTH)
+            keep = 1.0 / (1.0 + 4.0 * weight)
+            near = weight / (1.0 + 4.0 * weight)
 
             def widen(c, carry):
                 both = jnp.where((lane & 7) < 4, hrcv[0, g, c], hrcv[1, g, c])
@@ -282,35 +284,40 @@
 
             lax.fori_loop(0, CHUNKS, widen, 0)
 
-            def sweep(source, store):
-                def rows8(b, carry):
-                    start = 8 * b
-                    window = source(pl.ds(start, 10))
-                    middle = window[1:9].reshape(64, DEPTH)
-                    total = (window[0:8] + window[2:10]).reshape(64, DEPTH)
-                    total = total + (pltpu.roll(middle, 1, 1) + pltpu.roll(middle, DEPTH - 1, 1))
-                    base = ft[g, pl.ds(start + 1, 8)].reshape(64, DEPTH)
-                    store(start, (keep * base + near * total).reshape(8, 8, DEPTH))
-                    return carry
-
-                lax.fori_loop(0, ROWS // 8, rows8, 0)
+            def row(ref, r):
+                return [ref[r, :, 128 * t : 128 * t + 128] for t in range(3)]
+
+            def sweep(source, store, count):
+                up, middle = row(source, 0), row(source, 1)
+                for r in range(1, ROWS + 1):
+                    down = row(source, r + 1)
+                    base = row(ft.at[g], r)
+                    after = [pltpu.roll(t, 1, 1) for t in middle]
+                    before = [pltpu.roll(t, 127, 1) for t in middle]
+                    result = []
+                    for t in range(count):
+                        sides = jnp.where(lane == 0, after[(t + 2) % 3], after[t])
+                        sides = sides + jnp.where(lane == 127, before[(t + 1) % 3], before[t])
+                        result.append(keep * base[t] + near * ((up[t] + down[t]) + sides))
+                    store(r, result)
+                    up, middle = middle, down
 
             def into(ref):
-                def store(start, value):
-                    ref[pl.ds(start + 1, 8)] = value
+                def store(r, result):
+                    for t in range(3):
+                        ref[r, :, 128 * t : 128 * t + 128] = result[t]
 
                 return store
 
-            def last_store(start, value):
-                for i in range(8):
-                    rows = pl.ds(8 * g * ROWS + start + i, 8, stride=ROWS)
-                    fv[0, rows, :] = value[i, :, :128]
-                    fv[1, rows, :] = value[i, :, 128:COLS]
-
-            sweep(lambda rows: ft[g, rows], into(ita))
-            sweep(lambda rows: ita[rows], into(itb))
-            sweep(lambda rows: itb[rows], into(ita))
-            sweep(lambda rows: ita[rows], last_store)
+            def last_store(r, result):
+                rows = pl.ds(8 * g * ROWS + r - 1, 8, stride=ROWS)
+                fv[0, rows, :] = result[0]
+                fv[1, rows, :] = result[1]
+
+            sweep(ft.at[g], into(ita), 3)
+            sweep(ita, into(itb), 3)
+            sweep(itb, into(ita), 3)
+            sweep(ita, last_store, 2)
             return carry
 
         lax.fori_loop(first, last, tile, 0)
@@ -346,22 +353,22 @@
 
 
 def body(fields, evaluate, project, feed, kill):
-    rates = jnp.pad(jnp.stack([feed, feed + kill]), ((0, 0), (0, PADDED - POINTS)))
     items = CHUNKS + len(GROUPS) - 1
     partners = len(PARTNERS)
-    anywhere = pl.BlockSpec(memory_space=pl.ANY)
+    hbm = pl.BlockSpec(memory_space=pltpu.MemorySpace.HBM)
+    vmem = pl.BlockSpec(memory_space=pltpu.VMEM)
     dma = pltpu.SemaphoreType.DMA
     stepped = pl.pallas_call(
         kernel,
         out_shape=jax.ShapeDtypeStruct((2 * LOCAL, ROWS, COLS), F32),
-        in_specs=[anywhere, anywhere, anywhere, pl.BlockSpec(memory_space=pltpu.VMEM)],
-        out_specs=anywhere,
+        in_specs=[hbm, hbm, hbm, vmem, vmem],
+        out_specs=pl.BlockSpec(memory_space=pl.ANY),
         scratch_shapes=[
             pltpu.VMEM((2, 2 * LOCAL * ROWS, 128), F32),
             pltpu.VMEM((TILES, ROWS + 2, 8, DEPTH), F32),
             pltpu.VMEM((ROWS + 2, 8, DEPTH), F32),
             pltpu.VMEM((ROWS + 2, 8, DEPTH), F32),
-            pltpu.VMEM((POINTS, MODES), BF16),
+            pltpu.VMEM((MODES, POINTS), BF16),
             pltpu.VMEM((MODES, POINTS), BF16),
             pltpu.VMEM((4, POINTS, DEPTH), BF16),
             pltpu.VMEM((2, OUT_ROWS, PADDED), BF16),
@@ -386,12 +393,12 @@
             dma((len(GROUPS), 2)),
         ],
         compiler_params=pltpu.CompilerParams(
-            collective_id=0, has_side_effects=True, vmem_limit_bytes=60 * 2**20
+            collective_id=0, has_side_effects=True, vmem_limit_bytes=VMEM_LIMIT
         ),
         cost_estimate=pl.CostEstimate(
             flops=8 * 2 * LOCAL * ROWS * COLS * POINTS // 2, bytes_accessed=12 * 2**20, transcendentals=0
         ),
-    )(fields.reshape(2 * LOCAL, ROWS, COLS), evaluate, project, rates)
+    )(fields.reshape(2 * LOCAL, ROWS, COLS), evaluate.T, project, feed, kill)
     return stepped.reshape(2, LOCAL, ROWS, COLS)
 
 

time: 115 us -> 85.1 us (0.74)
  Pallas kernels: 105 us -> 79.8 us
  local copies, waits for them, and re-layouts: 8.21 us -> 5.1 us
  other arithmetic: 1.33 us -> 0 us
    pallas_call x1, Pallas kernels: 105 us -> 79.8 us  [body(): pl.pallas_call(kernel, out_shape=jax.ShapeDtypeStruct((2 * LOCAL, ROWS, C...]
    unnamed x2 -> x1, local copies, waits for them, and re-layouts: 7.5 us -> 5.1 us
where the time goes in v2:
time: 85.1 us; the launch traced here: 85 us
  Pallas kernels  79.8 us (94%)
  local copies, waits for them, and re-layouts  5.1 us (6%)
    pallas_call x1, Pallas kernels, body(): pl.pallas_call(kernel, out_shape=jax.ShapeDtypeStruct((2 * LOCAL, ROWS, C...  79.8 us
    unnamed x1, local copies, waits for them, and re-layouts  5.1 us

profile of v2, /device:TPU:0, one launch (start us, length us, event | category | flops | bytes accessed | tf_op | source)
XLA Modules:
  0.0 85.0 jit_solution(7997451491440965098)
XLA Ops:
  0.0 79.8 %shard_map.55 = f32[72,64,256]{2,1,0:T(8,128)} custom-call(f32[72,64,256]{2,1,0:T(8,128)} %bitcast.4, bf16[288,1584]{1,0:T(8,128)(2,1)} %bitcast.5, bf16[288,1584]{1,0:T(8,128)(2,1)} %project.1, f32[1584]{0:T(1024)} %feed.1, f32[1584]{0:T(1024)} %kill.1), custom_call_target="tpu_custom_call" | custom-call | flops 7474249728 | bytes 12582912 | tf_op jit(solution)/shard_map/pallas_call | solution.py:361
  79.8 5.1 %copy.7 = f32[2,36,64,256]{3,2,1,0:T(8,128)} copy(f32[2,36,64,256]{3,2,1,0:T(8,128)} %bitcast.3) | data formatting | bytes 9437184

commit v3 on v2

--- a/solution.py
+++ b/solution.py
@@ -23,7 +23,9 @@
 PADDED = 1664
 BLOCK = 528
 OUT_ROWS = 320
-GROUPS = ((0, 2), (2, 4), (4, 6), (6, 8), (8, 9))
+WINDOW = 3
+LAG = 2
+EARLY = 2
 PARTNERS = ((0, 1), (1, 0), (3, 0), (2, 0), (1, 1), (3, 1), (2, 1))
 
 
@@ -120,11 +122,11 @@
         own(chunk).start()
 
     for g in range(TILES):
-        ft[g, 0, :, :] = jnp.zeros((8, DEPTH), F32)
-        ft[g, ROWS + 1, :, :] = jnp.zeros((8, DEPTH), F32)
+        ft[g, 0, :, :] = jnp.zeros((8, COLS), F32)
+        ft[g, ROWS + 1, :, :] = jnp.zeros((8, COLS), F32)
     for ref in (ita, itb):
-        ref[0, :, :] = jnp.zeros((8, DEPTH), F32)
-        ref[ROWS + 1, :, :] = jnp.zeros((8, DEPTH), F32)
+        ref[0, :, :] = jnp.zeros((8, COLS), F32)
+        ref[ROWS + 1, :, :] = jnp.zeros((8, COLS), F32)
     for table in tables:
         table.wait()
     mode = iota((MODES, DEPTH), 0)
@@ -161,11 +163,12 @@
             column = jnp.sum(jnp.where(eye, jnp.broadcast_to(rate, (128, 128)), 0.0), axis=1, keepdims=True)
             rate_b[f, q : q + 128, :] = jnp.broadcast_to(column, (128, 128))
 
-    def react(chunk):
+    def arrive(chunk):
         for k in range(len(PARTNERS)):
             forward_in(chunk, k).wait_recv()
         own(chunk).wait()
 
+    def react(chunk):
         def block(b, carry):
             rows = pl.ds(pl.multiple_of(b * BLOCK, 16), BLOCK)
             feed = jnp.tile(rate_b[0, rows, :], (1, 2))
@@ -196,164 +199,195 @@
         mix = jnp.stack([mix[:, :COLS].reshape(8, 8, COLS), mix[:, COLS:].reshape(8, 8, COLS)], axis=1)
         bsnd[:, 4, chunk] = mix.astype(BF16).reshape(PARTS, 16, COLS)
 
-    def part_of(item, row):
-        first, last = GROUPS[max(0, item - 3)]
-        if item < CHUNKS:
-            return row[0].at[row[1], first:last, item]
-        return row[0].at[row[1], first:last]
-
-    def backward(item, k, incoming=False):
+    def backward(g, k, low=0, high=CHUNKS, incoming=False):
         part = partners[k]
         slot = part if incoming else me
         return pltpu.make_async_remote_copy(
-            src_ref=part_of(item, (bsnd, part)), dst_ref=part_of(item, (brcv, slot)),
-            send_sem=bs_sem.at[item, k], recv_sem=br_sem.at[item, slot],
+            src_ref=bsnd.at[part, g, low:high], dst_ref=brcv.at[slot, g, low:high],
+            send_sem=bs_sem.at[g, k], recv_sem=br_sem.at[g, slot],
             device_id=(part, col), device_id_type=MESH,
         )
 
-    def back_own(item):
-        return pltpu.make_async_copy(part_of(item, (bsnd, me)), part_of(item, (brcv, me)), bown_sem.at[item])
-
-    def send_back(item):
-        for k in range(len(PARTNERS)):
-            backward(item, k).start()
-        back_own(item).start()
-
-    items = CHUNKS + len(GROUPS) - 1
-    for chunk in range(CHUNKS):
+    def back_own(g, low=0, high=CHUNKS):
+        return pltpu.make_async_copy(bsnd.at[me, g, low:high], brcv.at[me, g, low:high], bown_sem.at[g])
+
+    def send_back(g, low=0, high=CHUNKS):
+        for k in range(len(PARTNERS)):
+            backward(g, k, low, high).start()
+        back_own(g, low, high).start()
+
+    def work(chunk):
         react(chunk)
         project_back(chunk)
-        send_back(chunk)
-    send_back(CHUNKS)
+
+    def early(chunk, carry):
+        arrive(chunk)
+        work(chunk)
+        return carry
+
+    lax.fori_loop(0, CHUNKS - 1, early, 0)
+    arrive(CHUNKS - 1)
+    for g in range(EARLY):
+        send_back(g, 0, CHUNKS - 1)
+    work(CHUNKS - 1)
+    for g in range(EARLY):
+        send_back(g, CHUNKS - 1, CHUNKS)
+    for g in range(EARLY, WINDOW):
+        send_back(g)
 
     lane = iota((8, 128), 1)
 
-    def gather(index):
-        first, last = GROUPS[index]
-        for item in range(CHUNKS) if index == 0 else (CHUNKS + index - 1,):
-            for k in range(len(PARTNERS)):
-                backward(item, k, True).wait_recv()
-            back_own(item).wait()
-        if index + 2 < len(GROUPS):
-            send_back(CHUNKS + index + 1)
-
-        def tile(g, carry):
-            def rows16(c, carry):
-                packed = jnp.zeros((8, 128), F32)
-                for s in range(PARTS):
-                    pair = brcv[s, g, c].astype(F32)
-                    for j in range(2):
-                        row = 16 * c + 2 * s + j + 1
-                        value = ft[g, row, :, :COLS] + TIME_STEP * pair[8 * j : 8 * j + 8]
-                        ft[g, row, :, :COLS] = value
-                        edge = jnp.where(lane < 64, value[:, :128], value[:, 128:])
-                        at = 2 * s + j
-                        packed = jnp.where((lane >> 3) == at, pltpu.roll(edge, (8 * at + 4) % 128, 1), packed)
-                hsnd[g, c] = packed
-                return carry
-
-            return lax.fori_loop(0, CHUNKS, rows16, carry)
-
-        lax.fori_loop(first, last, tile, 0)
-
-    def halo(index, side, incoming=False):
-        first, last = GROUPS[index]
+    def gather(g):
+        for k in range(len(PARTNERS)):
+            backward(g, k, incoming=True).wait_recv()
+        back_own(g).wait()
+
+        def rows16(c, carry):
+            packed = jnp.zeros((8, 128), F32)
+            for s in range(PARTS):
+                pair = brcv[s, g, c].astype(F32)
+                for j in range(2):
+                    row = 16 * c + 2 * s + j + 1
+                    value = ft[g, row, :, :COLS] + TIME_STEP * pair[8 * j : 8 * j + 8]
+                    ft[g, row, :, :COLS] = value
+                    edge = jnp.where(lane < 64, value[:, :128], value[:, 128:])
+                    at = 2 * s + j
+                    packed = jnp.where((lane >> 3) == at, pltpu.roll(edge, (8 * at + 4) % 128, 1), packed)
+            hsnd[g, c] = packed
+            return carry
+
+        lax.fori_loop(0, CHUNKS, rows16, 0)
+
+    def halo(g, side, incoming=False):
         there = 1 - side if incoming else side
         return pltpu.make_async_remote_copy(
-            src_ref=hsnd.at[first:last], dst_ref=hrcv.at[there, first:last],
-            send_sem=hs_sem.at[index, side], recv_sem=hr_sem.at[index, there],
+            src_ref=hsnd.at[g], dst_ref=hrcv.at[there, g],
+            send_sem=hs_sem.at[g, side], recv_sem=hr_sem.at[g, there],
             device_id=(me, left if side else right), device_id_type=MESH,
         )
 
-    def sweeps(index):
-        first, last = GROUPS[index]
+    def sweeps(g):
         for side in range(2):
-            halo(index, side, True).wait_recv()
-
-        def tile(g, carry):
-            pair = 8 * g + iota((8, 128), 0)
-            weight = jnp.where(pair < LOCAL, DIFFUSION[0], DIFFUSION[1])
-            keep = 1.0 / (1.0 + 4.0 * weight)
-            near = weight / (1.0 + 4.0 * weight)
-
-            def widen(c, carry):
-                both = jnp.where((lane & 7) < 4, hrcv[0, g, c], hrcv[1, g, c])
-                for at in range(16):
-                    ft[g, 16 * c + at + 1, :, COLS:] = pltpu.roll(both, (124 - 8 * at) % 128, 1)
-                return carry
-
-            lax.fori_loop(0, CHUNKS, widen, 0)
-
-            def row(ref, r):
-                return [ref[r, :, 128 * t : 128 * t + 128] for t in range(3)]
-
-            def sweep(source, store, count):
-                up, middle = row(source, 0), row(source, 1)
-                for r in range(1, ROWS + 1):
-                    down = row(source, r + 1)
-                    base = row(ft.at[g], r)
-                    after = [pltpu.roll(t, 1, 1) for t in middle]
-                    before = [pltpu.roll(t, 127, 1) for t in middle]
-                    result = []
-                    for t in range(count):
-                        sides = jnp.where(lane == 0, after[(t + 2) % 3], after[t])
-                        sides = sides + jnp.where(lane == 127, before[(t + 1) % 3], before[t])
-                        result.append(keep * base[t] + near * ((up[t] + down[t]) + sides))
-                    store(r, result)
-                    up, middle = middle, down
-
-            def into(ref):
-                def store(r, result):
-                    for t in range(3):
-                        ref[r, :, 128 * t : 128 * t + 128] = result[t]
-
-                return store
-
-            def last_store(r, result):
-                rows = pl.ds(8 * g * ROWS + r - 1, 8, stride=ROWS)
-                fv[0, rows, :] = result[0]
-                fv[1, rows, :] = result[1]
-
-            sweep(ft.at[g], into(ita), 3)
-            sweep(ita, into(itb), 3)
-            sweep(itb, into(ita), 3)
-            sweep(ita, last_store, 2)
-            return carry
-
-        lax.fori_loop(first, last, tile, 0)
-
-    def write(index, half):
-        first, last = GROUPS[index]
-        rows = pl.ds(8 * first, 8 * (last - first))
+            halo(g, side, True).wait_recv()
+        pair = 8 * g + iota((8, 128), 0)
+        weight = jnp.where(pair < LOCAL, DIFFUSION[0], DIFFUSION[1])
+        keep = 1.0 / (1.0 + 4.0 * weight)
+        near = weight / (1.0 + 4.0 * weight)
+
+        low = (lane & 7) < 4
+        lefts = [jnp.where(low, hrcv[0, g, c], hsnd[g, c]) for c in range(CHUNKS)]
+        rights = [jnp.where(low, hsnd[g, c], hrcv[1, g, c]) for c in range(CHUNKS)]
+        left_base, right_base = lefts, rights
+
+        def seam(now, base):
+            later = []
+            downs = [pltpu.roll(x, 8, 1) for x in now]
+            ups = [pltpu.roll(x, 120, 1) for x in now]
+            for c in range(CHUNKS):
+                total = jnp.where(lane < 8, downs[c - 1] if c else 0.0, downs[c])
+                total = total + jnp.where(lane >= 120, ups[c + 1] if c + 1 < CHUNKS else 0.0, ups[c])
+                total = total + (pltpu.roll(now[c], 1, 1) + pltpu.roll(now[c], 127, 1))
+                later.append(keep * base[c] + near * total)
+            return later
+
+        def row(ref, r):
+            return [ref[r, :, :128], ref[r, :, 128:]]
+
+        start = ft.at[g]
+
+        def sweep(source, store):
+            beside = [
+                jnp.where((lane & 7) == 3, x, pltpu.roll(y, 126, 1)) for x, y in zip(lefts, rights, strict=True)
+            ]
+            up, middle = row(source, 0), row(source, 1)
+            for r in range(1, ROWS + 1):
+                down = row(source, r + 1)
+                base = row(start, r) if source is not start else middle
+                after = [pltpu.roll(t, 1, 1) for t in middle]
+                before = [pltpu.roll(t, 127, 1) for t in middle]
+                edge = pltpu.roll(beside[(r - 1) // 16], (125 - 8 * ((r - 1) % 16)) % 128, 1)
+                sides = [
+                    jnp.where(lane == 0, edge, after[0]) + jnp.where(lane == 127, before[1], before[0]),
+                    jnp.where(lane == 0, after[0], after[1]) + jnp.where(lane == 127, edge, before[1]),
+                ]
+                store(r, [keep * base[t] + near * ((up[t] + down[t]) + sides[t]) for t in range(2)])
+                up, middle = middle, down
+
+        def into(ref):
+            def store(r, result):
+                ref[r, :, :128] = result[0]
+                ref[r, :, 128:] = result[1]
+
+            return store
+
+        def last_store(r, result):
+            rows = pl.ds(8 * g * ROWS + r - 1, 8, stride=ROWS)
+            fv[0, rows, :] = result[0]
+            fv[1, rows, :] = result[1]
+
+        source = start
+        for store_ref in (ita, itb, ita):
+            sweep(source, into(store_ref))
+            source = store_ref
+            lefts, rights = seam(lefts, left_base), seam(rights, right_base)
+        sweep(source, last_store)
+
+    def write(g, half):
+        rows = pl.ds(8 * g, 8)
         return pltpu.make_async_copy(
-            planes.at[half, rows], out.at[rows, :, pl.ds(128 * half, 128)], out_sem.at[index, half]
-        )
-
-    count = len(GROUPS)
-    for index in range(count + 1):
-        if index < count:
-            gather(index)
+            planes.at[half, rows], out.at[rows, :, pl.ds(128 * half, 128)], out_sem.at[g, half]
+        )
+
+    def turn(i, carry):
+        @pl.when(i < TILES)
+        def _():
+            gather(i)
             for side in range(2):
-                halo(index, side).start()
-        if index > 0:
-            sweeps(index - 1)
+                halo(i, side).start()
+
+        @pl.when(i + WINDOW < TILES)
+        def _():
+            send_back(i + WINDOW)
+
+        @pl.when(i >= LAG)
+        def _():
+            sweeps(i - LAG)
             for half in range(2):
-                write(index - 1, half).start()
+                write(i - LAG, half).start()
+
+        return carry
+
+    lax.fori_loop(0, TILES + LAG, turn, 0)
 
     for chunk in range(CHUNKS):
         for k in range(len(PARTNERS)):
             forward(chunk, k).wait_send()
-    for item in range(items):
-        for k in range(len(PARTNERS)):
-            backward(item, k).wait_send()
-    for index in range(count):
+
+    def finish(g, carry):
+        for k in range(len(PARTNERS)):
+            backward(g, k).wait_send()
         for side in range(2):
-            halo(index, side).wait_send()
-            write(index, side).wait()
+            halo(g, side).wait_send()
+            write(g, side).wait()
+        return carry
+
+    lax.fori_loop(0, TILES, finish, 0)
+
+
+def hand_over(source, target, held, in_sem, out_sem):
+    rows = [pl.ds(8 * g, 8) for g in range(TILES)]
+    reads = [pltpu.make_async_copy(source.at[r], held.at[r], in_sem.at[g]) for g, r in enumerate(rows)]
+    writes = [pltpu.make_async_copy(held.at[r], target.at[r], out_sem.at[g]) for g, r in enumerate(rows)]
+    for read in reads:
+        read.start()
+    for read, write in zip(reads, writes, strict=True):
+        read.wait()
+        write.start()
+    for write in writes:
+        write.wait()
 
 
 def body(fields, evaluate, project, feed, kill):
-    items = CHUNKS + len(GROUPS) - 1
     partners = len(PARTNERS)
     hbm = pl.BlockSpec(memory_space=pltpu.MemorySpace.HBM)
     vmem = pl.BlockSpec(memory_space=pltpu.VMEM)
@@ -365,9 +399,9 @@
         out_specs=pl.BlockSpec(memory_space=pl.ANY),
         scratch_shapes=[
             pltpu.VMEM((2, 2 * LOCAL * ROWS, 128), F32),
-            pltpu.VMEM((TILES, ROWS + 2, 8, DEPTH), F32),
-            pltpu.VMEM((ROWS + 2, 8, DEPTH), F32),
-            pltpu.VMEM((ROWS + 2, 8, DEPTH), F32),
+            pltpu.VMEM((TILES, ROWS + 2, 8, COLS), F32),
+            pltpu.VMEM((ROWS + 2, 8, COLS), F32),
+            pltpu.VMEM((ROWS + 2, 8, COLS), F32),
             pltpu.VMEM((MODES, POINTS), BF16),
             pltpu.VMEM((MODES, POINTS), BF16),
             pltpu.VMEM((4, POINTS, DEPTH), BF16),
@@ -382,15 +416,15 @@
             pltpu.VMEM((2, TILES, CHUNKS, 8, 128), F32),
             dma((CHUNKS, 2)),
             dma((2,)),
-            dma((len(GROUPS), 2)),
+            dma((TILES, 2)),
             dma((CHUNKS,)),
             dma((CHUNKS, partners)),
             dma((CHUNKS, PARTS)),
-            dma((items,)),
-            dma((items, partners)),
-            dma((items, PARTS)),
-            dma((len(GROUPS), 2)),
-            dma((len(GROUPS), 2)),
+            dma((TILES,)),
+            dma((TILES, partners)),
+            dma((TILES, PARTS)),
+            dma((TILES, 2)),
+            dma((TILES, 2)),
         ],
         compiler_params=pltpu.CompilerParams(
             collective_id=0, has_side_effects=True, vmem_limit_bytes=VMEM_LIMIT
@@ -399,6 +433,14 @@
             flops=8 * 2 * LOCAL * ROWS * COLS * POINTS // 2, bytes_accessed=12 * 2**20, transcendentals=0
         ),
     )(fields.reshape(2 * LOCAL, ROWS, COLS), evaluate.T, project, feed, kill)
+    stepped = pl.pallas_call(
+        hand_over,
+        out_shape=jax.ShapeDtypeStruct((2 * LOCAL, ROWS, COLS), F32),
+        in_specs=[hbm],
+        out_specs=hbm,
+        scratch_shapes=[pltpu.VMEM((2 * LOCAL, ROWS, COLS), F32), dma((TILES,)), dma((TILES,))],
+        compiler_params=pltpu.CompilerParams(vmem_limit_bytes=VMEM_LIMIT),
+    )(stepped)
     return stepped.reshape(2, LOCAL, ROWS, COLS)
 
 

time: 85.1 us -> 79.5 us (0.934)
  local copies, waits for them, and re-layouts: 5.1 us -> 0 us
    unnamed x1 -> x0, local copies, waits for them, and re-layouts: 5.1 us -> none
    pallas_call x1, Pallas kernels: 79.8 us -> 75.1 us  [body(): pl.pallas_call(kernel, out_shape=jax.ShapeDtypeStruct((2 * LOCAL, ROWS, C...]
    pallas_call x0 -> x1, Pallas kernels: none -> 4.16 us  [body(): pl.pallas_call(hand_over, out_shape=jax.ShapeDtypeStruct((2 * LOCAL, ROWS...]
where the time goes in v3:
time: 79.5 us; the launch traced here: 79.3 us
  Pallas kernels  79.3 us (100%)
    pallas_call x1, Pallas kernels, body(): pl.pallas_call(kernel, out_shape=jax.ShapeDtypeStruct((2 * LOCAL, ROWS, C...  75.1 us
    pallas_call x1, Pallas kernels, body(): pl.pallas_call(hand_over, out_shape=jax.ShapeDtypeStruct((2 * LOCAL, ROWS...  4.16 us

profile of v3, /device:TPU:0, one launch (start us, length us, event | category | flops | bytes accessed | tf_op | source)
XLA Modules:
  0.0 79.3 jit_solution(10115474502202751846)
XLA Ops:
  0.0 75.1 %shard_map.55.source = f32[72,64,256]{2,1,0:T(8,128)} custom-call(f32[72,64,256]{2,1,0:T(8,128)} %bitcast.3, bf16[288,1584]{1,0:T(8,128)(2,1)} %bitcast.4, bf16[288,1584]{1,0:T(8,128)(2,1)} %project.1, f32[1584]{0:T(1024)} %feed.1, f32[1584]{0:T(1024)} %kill.1), custom_call_target="tpu_custom_call" | custom-call | flops 7474249728 | bytes 12582912 | tf_op jit(solution)/shard_map/pallas_call | solution.py:395
  75.1 4.2 %shard_map.56 = f32[72,64,256]{2,1,0:T(8,128)} custom-call(f32[72,64,256]{2,1,0:T(8,128)} %shard_map.55.source), custom_call_target="tpu_custom_call" | custom-call | tf_op jit(solution)/shard_map/pallas_call | solution.py:436

commit v4 on v3

--- a/solution.py
+++ b/solution.py
@@ -25,6 +25,8 @@
 OUT_ROWS = 320
 WINDOW = 3
 LAG = 2
+LATE = 1
+SWEPT = TILES - LATE
 EARLY = 2
 PARTNERS = ((0, 1), (1, 0), (3, 0), (2, 0), (1, 1), (3, 1), (2, 1))
 
@@ -33,11 +35,75 @@
     return lax.broadcasted_iota(jnp.int32, shape, dim)
 
 
+def sweep_tile(g, start, own_edge, left_edge, right_edge, ita, itb, fv, place):
+    lane = iota((8, 128), 1)
+    pair = 8 * g + iota((8, 128), 0)
+    weight = jnp.where(pair < LOCAL, DIFFUSION[0], DIFFUSION[1])
+    keep = 1.0 / (1.0 + 4.0 * weight)
+    near = weight / (1.0 + 4.0 * weight)
+
+    low = (lane & 7) < 4
+    lefts = [jnp.where(low, left_edge[c], own_edge[c]) for c in range(CHUNKS)]
+    rights = [jnp.where(low, own_edge[c], right_edge[c]) for c in range(CHUNKS)]
+    left_base, right_base = lefts, rights
+
+    def seam(now, base):
+        later = []
+        downs = [pltpu.roll(x, 8, 1) for x in now]
+        ups = [pltpu.roll(x, 120, 1) for x in now]
+        for c in range(CHUNKS):
+            total = jnp.where(lane < 8, downs[c - 1] if c else 0.0, downs[c])
+            total = total + jnp.where(lane >= 120, ups[c + 1] if c + 1 < CHUNKS else 0.0, ups[c])
+            total = total + (pltpu.roll(now[c], 1, 1) + pltpu.roll(now[c], 127, 1))
+            later.append(keep * base[c] + near * total)
+        return later
+
+    def row(ref, r):
+        return [ref[r, :, :128], ref[r, :, 128:]]
+
+    def sweep(source, store):
+        beside = [
+            jnp.where((lane & 7) == 3, x, pltpu.roll(y, 126, 1)) for x, y in zip(lefts, rights, strict=True)
+        ]
+        up, middle = row(source, 0), row(source, 1)
+        for r in range(1, ROWS + 1):
+            down = row(source, r + 1)
+            base = row(start, r) if source is not start else middle
+            after = [pltpu.roll(t, 1, 1) for t in middle]
+            before = [pltpu.roll(t, 127, 1) for t in middle]
+            edge = pltpu.roll(beside[(r - 1) // 16], (125 - 8 * ((r - 1) % 16)) % 128, 1)
+            sides = [
+                jnp.where(lane == 0, edge, after[0]) + jnp.where(lane == 127, before[1], before[0]),
+                jnp.where(lane == 0, after[0], after[1]) + jnp.where(lane == 127, edge, before[1]),
+            ]
+            store(r, [keep * base[t] + near * ((up[t] + down[t]) + sides[t]) for t in range(2)])
+            up, middle = middle, down
+
+    def into(ref):
+        def store(r, result):
+            ref[r, :, :128] = result[0]
+            ref[r, :, 128:] = result[1]
+
+        return store
+
+    def last_store(r, result):
+        rows = pl.ds(8 * place * ROWS + r - 1, 8, stride=ROWS)
+        fv[0, rows, :] = result[0]
+        fv[1, rows, :] = result[1]
+
+    source = start
+    for store_ref in (ita, itb, ita):
+        sweep(source, into(store_ref))
+        source = store_ref
+        lefts, rights = seam(lefts, left_base), seam(rights, right_base)
+    sweep(source, last_store)
+
+
 def kernel(
-    fields, evaluate, project, feed, kill, out,
+    fields, evaluate, project, feed, kill, out, rs_out, edge_out,
     fv, ft, ita, itb, ev, pj, weights, proj, rate_b,
     snd, rcv, reacted, bsnd, brcv, hsnd, hrcv,
-    in_sem, table_sem, out_sem, own_sem, fs_sem, fr_sem, bown_sem, bs_sem, br_sem, hs_sem, hr_sem,
+    in_sem, table_sem, out_sem, own_sem, fs_sem, fr_sem, bown_sem, bs_sem, br_sem, hs_sem, hr_sem, late_sem,
 ):
     me, col = lax.axis_index("mode"), lax.axis_index("col")
     cols = lax.axis_size("col")
@@ -269,68 +335,10 @@
     def sweeps(g):
         for side in range(2):
             halo(g, side, True).wait_recv()
-        pair = 8 * g + iota((8, 128), 0)
-        weight = jnp.where(pair < LOCAL, DIFFUSION[0], DIFFUSION[1])
-        keep = 1.0 / (1.0 + 4.0 * weight)
-        near = weight / (1.0 + 4.0 * weight)
-
-        low = (lane & 7) < 4
-        lefts = [jnp.where(low, hrcv[0, g, c], hsnd[g, c]) for c in range(CHUNKS)]
-        rights = [jnp.where(low, hsnd[g, c], hrcv[1, g, c]) for c in range(CHUNKS)]
-        left_base, right_base = lefts, rights
-
-        def seam(now, base):
-            later = []
-            downs = [pltpu.roll(x, 8, 1) for x in now]
-            ups = [pltpu.roll(x, 120, 1) for x in now]
-            for c in range(CHUNKS):
-                total = jnp.where(lane < 8, downs[c - 1] if c else 0.0, downs[c])
-                total = total + jnp.where(lane >= 120, ups[c + 1] if c + 1 < CHUNKS else 0.0, ups[c])
-                total = total + (pltpu.roll(now[c], 1, 1) + pltpu.roll(now[c], 127, 1))
-                later.append(keep * base[c] + near * total)
-            return later
-
-        def row(ref, r):
-            return [ref[r, :, :128], ref[r, :, 128:]]
-
-        start = ft.at[g]
-
-        def sweep(source, store):
-            beside = [
-                jnp.where((lane & 7) == 3, x, pltpu.roll(y, 126, 1)) for x, y in zip(lefts, rights, strict=True)
-            ]
-            up, middle = row(source, 0), row(source, 1)
-            for r in range(1, ROWS + 1):
-                down = row(source, r + 1)
-                base = row(start, r) if source is not start else middle
-                after = [pltpu.roll(t, 1, 1) for t in middle]
-                before = [pltpu.roll(t, 127, 1) for t in middle]
-                edge = pltpu.roll(beside[(r - 1) // 16], (125 - 8 * ((r - 1) % 16)) % 128, 1)
-                sides = [
-                    jnp.where(lane == 0, edge, after[0]) + jnp.where(lane == 127, before[1], before[0]),
-                    jnp.where(lane == 0, after[0], after[1]) + jnp.where(lane == 127, edge, before[1]),
-                ]
-                store(r, [keep * base[t] + near * ((up[t] + down[t]) + sides[t]) for t in range(2)])
-                up, middle = middle, down
-
-        def into(ref):
-            def store(r, result):
-                ref[r, :, :128] = result[0]
-                ref[r, :, 128:] = result[1]
-
-            return store
-
-        def last_store(r, result):
-            rows = pl.ds(8 * g * ROWS + r - 1, 8, stride=ROWS)
-            fv[0, rows, :] = result[0]
-            fv[1, rows, :] = result[1]
-
-        source = start
-        for store_ref in (ita, itb, ita):
-            sweep(source, into(store_ref))
-            source = store_ref
-            lefts, rights = seam(lefts, left_base), seam(rights, right_base)
-        sweep(source, last_store)
+        own_edge, left_edge, right_edge = [
+            [part[c] for c in range(CHUNKS)] for part in (hsnd.at[g], hrcv.at[0, g], hrcv.at[1, g])
+        ]
+        sweep_tile(g, ft.at[g], own_edge, left_edge, right_edge, ita, itb, fv, g)
 
     def write(g, half):
         rows = pl.ds(8 * g, 8)
@@ -357,7 +365,19 @@
 
         return carry
 
-    lax.fori_loop(0, TILES + LAG, turn, 0)
+    lax.fori_loop(0, TILES + LAG - LATE, turn, 0)
+
+    late = [pltpu.make_async_copy(ft.at[SWEPT:], rs_out, late_sem.at[0])]
+    late.append(pltpu.make_async_copy(hsnd.at[SWEPT:], edge_out.at[0], late_sem.at[1]))
+    for side in range(2):
+        late.append(pltpu.make_async_copy(hrcv.at[side, SWEPT:], edge_out.at[1 + side], late_sem.at[2 + side]))
+    for copy in late[:2]:
+        copy.start()
+    for g in range(SWEPT, TILES):
+        for side in range(2):
+            halo(g, side, True).wait_recv()
+    for copy in late[2:]:
+        copy.start()
 
     for chunk in range(CHUNKS):
         for k in range(len(PARTNERS)):
@@ -368,23 +388,48 @@
             backward(g, k).wait_send()
         for side in range(2):
             halo(g, side).wait_send()
-            write(g, side).wait()
+
+        @pl.when(g < SWEPT)
+        def _():
+            for half in range(2):
+                write(g, half).wait()
+
         return carry
 
     lax.fori_loop(0, TILES, finish, 0)
-
-
-def hand_over(source, target, held, in_sem, out_sem):
+    for copy in late:
+        copy.wait()
+
+
+def hand_over(source, rs, edges, target, held, ft, near, ita, itb, fv, in_sem, late_sem, out_sem, done_sem):
+    first = [pltpu.make_async_copy(rs, ft, late_sem.at[0]), pltpu.make_async_copy(edges, near, late_sem.at[1])]
     rows = [pl.ds(8 * g, 8) for g in range(TILES)]
-    reads = [pltpu.make_async_copy(source.at[r], held.at[r], in_sem.at[g]) for g, r in enumerate(rows)]
-    writes = [pltpu.make_async_copy(held.at[r], target.at[r], out_sem.at[g]) for g, r in enumerate(rows)]
-    for read in reads:
-        read.start()
+    reads = [pltpu.make_async_copy(source.at[rows[g]], held.at[rows[g]], in_sem.at[g]) for g in range(SWEPT)]
+    writes = [pltpu.make_async_copy(held.at[rows[g]], target.at[rows[g]], out_sem.at[g]) for g in range(SWEPT)]
+    for copy in first + reads:
+        copy.start()
+    for ref in (ita, itb):
+        ref[0, :, :] = jnp.zeros((8, COLS), F32)
+        ref[ROWS + 1, :, :] = jnp.zeros((8, COLS), F32)
+    for copy in first:
+        copy.wait()
     for read, write in zip(reads, writes, strict=True):
         read.wait()
         write.start()
-    for write in writes:
-        write.wait()
+    planes = fv.reshape(2, 8 * LATE, ROWS, 128)
+    last = []
+    for i in range(LATE):
+        own_edge, left_edge, right_edge = [[near[k, i, c] for c in range(CHUNKS)] for k in range(3)]
+        sweep_tile(SWEPT + i, ft.at[i], own_edge, left_edge, right_edge, ita, itb, fv, i)
+        for half in range(2):
+            lanes = pl.ds(128 * half, 128)
+            copy = pltpu.make_async_copy(
+                planes.at[half, pl.ds(8 * i, 8)], target.at[rows[SWEPT + i], :, lanes], done_sem.at[i, half]
+            )
+            copy.start()
+            last.append(copy)
+    for copy in writes + last:
+        copy.wait()
 
 
 def body(fields, evaluate, project, feed, kill):
@@ -392,11 +437,15 @@
     hbm = pl.BlockSpec(memory_space=pltpu.MemorySpace.HBM)
     vmem = pl.BlockSpec(memory_space=pltpu.VMEM)
     dma = pltpu.SemaphoreType.DMA
-    stepped = pl.pallas_call(
+    stepped, rs, edges = pl.pallas_call(
         kernel,
-        out_shape=jax.ShapeDtypeStruct((2 * LOCAL, ROWS, COLS), F32),
+        out_shape=[
+            jax.ShapeDtypeStruct((2 * LOCAL, ROWS, COLS), F32),
+            jax.ShapeDtypeStruct((LATE, ROWS + 2, 8, COLS), F32),
+            jax.ShapeDtypeStruct((3, LATE, CHUNKS, 8, 128), F32),
+        ],
         in_specs=[hbm, hbm, hbm, vmem, vmem],
-        out_specs=pl.BlockSpec(memory_space=pl.ANY),
+        out_specs=[hbm] * 3,
         scratch_shapes=[
             pltpu.VMEM((2, 2 * LOCAL * ROWS, 128), F32),
             pltpu.VMEM((TILES, ROWS + 2, 8, COLS), F32),
@@ -425,6 +474,7 @@
             dma((TILES, PARTS)),
             dma((TILES, 2)),
             dma((TILES, 2)),
+            dma((4,)),
         ],
         compiler_params=pltpu.CompilerParams(
             collective_id=0, has_side_effects=True, vmem_limit_bytes=VMEM_LIMIT
@@ -436,11 +486,22 @@
     stepped = pl.pallas_call(
         hand_over,
         out_shape=jax.ShapeDtypeStruct((2 * LOCAL, ROWS, COLS), F32),
-        in_specs=[hbm],
+        in_specs=[hbm] * 3,
         out_specs=hbm,
-        scratch_shapes=[pltpu.VMEM((2 * LOCAL, ROWS, COLS), F32), dma((TILES,)), dma((TILES,))],
+        scratch_shapes=[
+            pltpu.VMEM((2 * LOCAL, ROWS, COLS), F32),
+            pltpu.VMEM((LATE, ROWS + 2, 8, COLS), F32),
+            pltpu.VMEM((3, LATE, CHUNKS, 8, 128), F32),
+            pltpu.VMEM((ROWS + 2, 8, COLS), F32),
+            pltpu.VMEM((ROWS + 2, 8, COLS), F32),
+            pltpu.VMEM((2, 8 * LATE * ROWS, 128), F32),
+            dma((SWEPT,)),
+            dma((2,)),
+            dma((SWEPT,)),
+            dma((LATE, 2)),
+        ],
         compiler_params=pltpu.CompilerParams(vmem_limit_bytes=VMEM_LIMIT),
-    )(stepped)
+    )(stepped, rs, edges)
     return stepped.reshape(2, LOCAL, ROWS, COLS)
 
 

time: 79.5 us -> 78.9 us (level)
    pallas_call x1, Pallas kernels: 75.1 us -> 73.3 us  [body(): pl.pallas_call(kernel, out_shape=[jax.ShapeDtypeStruct((2 * LOCAL, ROWS,...]
    pallas_call x1, Pallas kernels: 4.16 us -> 5.46 us  [body(): pl.pallas_call(hand_over, out_shape=jax.ShapeDtypeStruct((2 * LOCAL, ROWS...]
where the time goes in v4:
time: 78.9 us; the launch traced here: 78.8 us
  Pallas kernels  78.7 us (100%)
    pallas_call x1, Pallas kernels, body(): pl.pallas_call(kernel, out_shape=[jax.ShapeDtypeStruct((2 * LOCAL, ROWS,...  73.3 us
    pallas_call x1, Pallas kernels, body(): pl.pallas_call(hand_over, out_shape=jax.ShapeDtypeStruct((2 * LOCAL, ROWS...  5.46 us

profile of v4, /device:TPU:0, one launch (start us, length us, event | category | flops | bytes accessed | tf_op | source)
XLA Modules:
  0.0 78.8 jit_solution(12321518940584959732)
XLA Ops:
  0.0 73.3 %shard_map.55 = (f32[72,64,256]{2,1,0:T(8,128)}, f32[1,66,8,256]{3,2,1,0:T(8,128)}, f32[3,1,4,8,128]{4,3,2,1,0:T(8,128)}) custom-call(f32[72,64,256]{2,1,0:T(8,128)} %bitcast.3, bf16[288,1584]{1,0:T(8,128)(2,1)} %bitcast.4, bf16[288,1584]{1,0:T(8,128)(2,1)} %project.1, f32[1584]{0:T(1024)} %feed.1, f32[1584]{0:T(1024)} %kill.1), custom_call_target="tpu_custom_call" | custom-call | flops 7474249728 | bytes 12582912 | tf_op jit(solution)/shard_map/pallas_call | solution.py:440
  73.3 5.5 %shard_map.56 = f32[72,64,256]{2,1,0:T(8,128)} custom-call(f32[72,64,256]{2,1,0:T(8,128)} %get-tuple-element.8.source, f32[1,66,8,256]{3,2,1,0:T(8,128)} %get-tuple-element.9.rs, f32[3,1,4,8,128]{4,3,2,1,0:T(8,128)} %get-tuple-element.10.edges), custom_call_target="tpu_custom_call" | custom-call | tf_op jit(solution)/shard_map/pallas_call | solution.py:486

commit v5 on v4

--- a/solution.py
+++ b/solution.py
@@ -27,7 +27,7 @@
 LAG = 2
 LATE = 1
 SWEPT = TILES - LATE
-EARLY = 2
+EARLY = 3
 PARTNERS = ((0, 1), (1, 0), (3, 0), (2, 0), (1, 1), (3, 1), (2, 1))
 
 

time: 78.9 us -> 79.8 us (1.011); the launches traced: 78.8 us -> 78.6 us
  no operation moved by 1% of the time
where the time goes in v5:
time: 79.8 us; the launch traced here: 78.6 us
  Pallas kernels  78.5 us (98%)
    pallas_call x1, Pallas kernels, body(): pl.pallas_call(kernel, out_shape=[jax.ShapeDtypeStruct((2 * LOCAL, ROWS,...  73.1 us
    pallas_call x1, Pallas kernels, body(): pl.pallas_call(hand_over, out_shape=jax.ShapeDtypeStruct((2 * LOCAL, ROWS...  5.46 us

profile of v5, /device:TPU:0, one launch (start us, length us, event | category | flops | bytes accessed | tf_op | source)
XLA Modules:
  0.0 78.6 jit_solution(14395554231753142083)
XLA Ops:
  0.0 73.1 %shard_map.55 = (f32[72,64,256]{2,1,0:T(8,128)}, f32[1,66,8,256]{3,2,1,0:T(8,128)}, f32[3,1,4,8,128]{4,3,2,1,0:T(8,128)}) custom-call(f32[72,64,256]{2,1,0:T(8,128)} %bitcast.3, bf16[288,1584]{1,0:T(8,128)(2,1)} %bitcast.4, bf16[288,1584]{1,0:T(8,128)(2,1)} %project.1, f32[1584]{0:T(1024)} %feed.1, f32[1584]{0:T(1024)} %kill.1), custom_call_target="tpu_custom_call" | custom-call | flops 7474249728 | bytes 12582912 | tf_op jit(solution)/shard_map/pallas_call | solution.py:440
  73.1 5.5 %shard_map.56 = f32[72,64,256]{2,1,0:T(8,128)} custom-call(f32[72,64,256]{2,1,0:T(8,128)} %get-tuple-element.8.source, f32[1,66,8,256]{3,2,1,0:T(8,128)} %get-tuple-element.9.rs, f32[3,1,4,8,128]{4,3,2,1,0:T(8,128)} %get-tuple-element.10.edges), custom_call_target="tpu_custom_call" | custom-call | tf_op jit(solution)/shard_map/pallas_call | solution.py:486
